TPU v7x, 256 devices: a whole 4x4x8 slice. The times are simulated.
256 devices in a mesh: batch: 16 (over z, core), proto: 16 (over y, x).
Axes of the slice: x: 4, y: 4, z: 8, core: 2. Of those that a mesh axis runs over, the one named last changes fastest.
Arguments:
- student_features: bfloat16 [10, 2048, 256], P(None, 'batch'), may hold values from -8 to 8
- teacher_features: bfloat16 [2, 2048, 256], P(None, 'batch'), may hold values from -8 to 8
- student_prototypes: bfloat16 [256, 65536], P(None, 'proto'), may hold values from -0.5 to 0.5
- teacher_prototypes: bfloat16 [256, 65536], P(None, 'proto'), may hold values from -0.5 to 0.5
Outputs:
- mean_loss: float32 [], replicated
- grad_features: float32 [10, 2048, 256], P(None, ('batch', 'proto'))
- grad_prototypes: float32 [256, 65536], P('batch', 'proto')
All inputs are finite; a program needn't handle non-finite values.
Results may differ from a plain program's by a relative error of at most 0.001.
The roundings to bfloat16 on the way count: a program that leaves them out, or rounds other values in their place, can miss the bound.
Values sent between devices are 32-bit elements; how exact they have to be, the bound alone decides.
A program may use at most 192 MiB of HBM per device.

v0:
```python
import jax
import jax.numpy as jnp
from jax import lax
from jax.sharding import PartitionSpec as P

CLUSTER_NUMBER = 65536
WIDE_CROP_NUMBER = 2
SK_ITERS = 3
PAIRS = 18


STUDENT_TEMP = 0.1
TEACHER_TEMP = 0.07
NORM_EPS = 1e-06


def unit_rows(values):
    floats = values.astype(jnp.float32)
    inverse = lax.rsqrt(jnp.sum(floats * floats, axis=-1, keepdims=True) + NORM_EPS)
    return (floats * inverse, inverse)


def unit_columns(values):
    floats = values.astype(jnp.float32)
    inverse = lax.rsqrt(jnp.sum(floats * floats, axis=0, keepdims=True) + NORM_EPS)
    return (floats * inverse, inverse)


def proto_step(cluster_share):
    column_mass = lax.psum(jnp.sum(cluster_share, axis=0), "batch")
    return cluster_share / (CLUSTER_NUMBER * column_mass[None, :])


def full_sweep(cluster_share, sample_number):
    cluster_share = proto_step(cluster_share)
    row_mass = lax.psum(jnp.sum(cluster_share, axis=1), "proto")
    return cluster_share / (sample_number * row_mass[:, None])


def on_device(student_features, teacher_features, student_prototypes, teacher_prototypes):
    crop_count, img_local, feature_dim = student_features.shape
    proto_local = student_prototypes.shape[1]
    batch_devices = lax.axis_size("batch")
    proto_devices = lax.axis_size("proto")
    images_all = img_local * batch_devices
    teacher_rows = WIDE_CROP_NUMBER * images_all
    student_count = crop_count * img_local
    unit_student, student_scale = unit_rows(student_features)
    student_bf = unit_student.astype(jnp.bfloat16).reshape(student_count, feature_dim)
    unit_proto, proto_scale = unit_columns(student_prototypes)
    proto_bf = unit_proto.astype(jnp.bfloat16)
    unit_teacher, unused_scale = unit_rows(teacher_features)
    teacher_bf = unit_teacher.astype(jnp.bfloat16).reshape(
        WIDE_CROP_NUMBER * img_local, feature_dim
    )
    unit_tproto, unused_tscale = unit_columns(teacher_prototypes)
    teacher_proto_bf = unit_tproto.astype(jnp.bfloat16)
    cluster_share = jnp.exp(
        jnp.dot(teacher_bf, teacher_proto_bf, preferred_element_type=jnp.float32) / TEACHER_TEMP
    )
    logits = jnp.dot(student_bf, proto_bf, preferred_element_type=jnp.float32) / STUDENT_TEMP
    exp_partial = jnp.sum(jnp.exp(logits), axis=1)
    for sweep_index in range(SK_ITERS):
        cluster_share = full_sweep(cluster_share, teacher_rows)
    exp_total = lax.psum(exp_partial, "proto")
    cluster_targets_matrix = (teacher_rows * cluster_share).reshape(
        WIDE_CROP_NUMBER, img_local, proto_local
    )
    first_global = cluster_targets_matrix[0]
    second_global = cluster_targets_matrix[1]
    summed = first_global + second_global
    targets = jnp.concatenate(
        [
            second_global[None],
            first_global[None],
            jnp.broadcast_to(summed[None], (crop_count - 2, img_local, proto_local)),
        ],
        axis=0,
    )
    pair_count = jnp.where(jnp.arange(crop_count) < 2, jnp.float32(1.0), jnp.float32(2.0))[
        :, None, None
    ]
    log_norm = jnp.log(exp_total).reshape(crop_count, img_local, 1)
    logits_crop = logits.reshape(crop_count, img_local, proto_local)
    loss_part = jnp.sum(targets * (log_norm - logits_crop))
    mean_loss = lax.psum(loss_part, ("batch", "proto")) / (images_all * PAIRS)
    factor = 1.0 / (images_all * PAIRS * STUDENT_TEMP)
    grad_cos = ((pair_count * jnp.exp(logits_crop - log_norm) - targets) * factor).astype(
        jnp.bfloat16
    )
    grad_cos = grad_cos.reshape(student_count, proto_local)
    feature_cot = lax.dot_general(
        grad_cos, proto_bf, (((1,), (1,)), ((), ())), preferred_element_type=jnp.float32
    )
    feature_cot = feature_cot.reshape(crop_count, img_local, feature_dim)
    own_count = img_local // proto_devices
    own_start = lax.axis_index("proto") * own_count
    cot_total = lax.psum(feature_cot, "proto")
    cot_own = lax.dynamic_slice_in_dim(cot_total, own_start, own_count, 1)
    unit_own = lax.dynamic_slice_in_dim(unit_student, own_start, own_count, 1)
    scale_own = lax.dynamic_slice_in_dim(student_scale, own_start, own_count, 1)
    grad_features = scale_own * (
        cot_own - unit_own * jnp.sum(unit_own * cot_own, axis=-1, keepdims=True)
    )
    curvature = jnp.sum(logits * STUDENT_TEMP * grad_cos.astype(jnp.float32), axis=0)
    rows_here = feature_dim // batch_devices
    product = lax.dot_general(
        student_bf, grad_cos, (((0,), (0,)), ((), ())), preferred_element_type=jnp.float32
    )
    term_total = lax.psum(product - unit_proto * curvature[None, :], "batch")
    term_own = lax.dynamic_slice_in_dim(
        term_total, lax.axis_index("batch") * rows_here, rows_here, 0
    )
    grad_prototypes = proto_scale * term_own
    return (mean_loss, grad_features, grad_prototypes)


def solution(mesh):
    placed = (P(None, "batch", None), P(None, "batch", None), P(None, "proto"), P(None, "proto"))
    return jax.shard_map(
        on_device,
        mesh=mesh,
        in_specs=placed,
        out_specs=(P(), P(None, ("batch", "proto"), None), P("batch", "proto")),
        check_vma=False,
    )
```

profile of v0, /device:TPU:32, one launch (start us, length us, event | category | flops | bytes accessed | tf_op | source)
XLA Modules:
  0.0 583.0 jit_solution(13375280952865046598)
XLA Ops:
  7.2 1.0 fusion.36
  8.3 1.0 fusion.37
  9.3 2.0 fusion.16
  11.3 4.6 fusion.46
  16.0 47.5 %psum.70 = f32[4096]{0:T(1024)S(1)} all-reduce(f32[4096]{0:T(1024)S(1)} %get-tuple-element.17), channel_id=1, replica_groups=mesh['batch'=16,'proto'=16] {'batch'}, use_global_device_ids=true, to_apply=%region_3.0 | all-reduce | flops 4096 | bytes 32768 | tf_op jit(solution)/shard_map/psum | solution.py:30
  63.4 2.6 divide_reduce_fusion
  66.0 40.7 %psum.71 = f32[256]{0:T(256)S(1)} all-reduce(f32[256]{0:T(256)S(1)} %divide_reduce_fusion), channel_id=1, replica_groups=mesh['batch'=16,'proto'=16] {'proto'}, use_global_device_ids=true, to_apply=%region_5.0 | all-reduce | flops 256 | bytes 2048 | tf_op jit(solution)/shard_map/psum | solution.py:36
  106.7 3.0 fusion.21
  109.7 45.7 %psum.72 = f32[4096]{0:T(1024)S(1)} all-reduce(f32[4096]{0:T(1024)S(1)} %fusion.21), channel_id=1, replica_groups=mesh['batch'=16,'proto'=16] {'batch'}, use_global_device_ids=true, to_apply=%region_7.0 | all-reduce | flops 4096 | bytes 32768 | tf_op jit(solution)/shard_map/psum | solution.py:30
  155.4 3.0 fusion.22
  158.4 35.5 %psum.73 = f32[256]{0:T(256)S(1)} all-reduce(f32[256]{0:T(256)S(1)} %fusion.22), channel_id=1, replica_groups=mesh['batch'=16,'proto'=16] {'proto'}, use_global_device_ids=true, to_apply=%region_9.0 | all-reduce | flops 256 | bytes 2048 | tf_op jit(solution)/shard_map/psum | solution.py:36
  193.9 3.2 fusion.23
  197.1 45.8 %psum.74 = f32[4096]{0:T(1024)S(1)} all-reduce(f32[4096]{0:T(1024)S(1)} %fusion.23), channel_id=1, replica_groups=mesh['batch'=16,'proto'=16] {'batch'}, use_global_device_ids=true, to_apply=%region_11.0 | all-reduce | flops 4096 | bytes 32768 | tf_op jit(solution)/shard_map/psum | solution.py:30
  242.9 3.4 fusion.24
  246.3 0.2 fusion.32
  246.6 1.3 convert_multiply_fusion.4
  247.9 0.4 fusion.18
  248.3 15.4 %broadcast_multiply_fusion = (f32[1280,4096]{1,0:T(8,128)}, f32[1280]{0:T(1024)S(1)}, f32[1280,4096]{1,0:T(8,128)}) fusion(bf16[1280,256]{1,0:T(8,128)(2,1)S(1)} %bitcast.37, bf16[256,4096]{1,0:T(8,128)(2,1)S(1)} %copy-done.1, f32[4096]{0:T(1024)S(1)} %add_rsqrt_fusion), kind=kOutput, calls=%fused_computation.10 | convolution fusion | flops 2697984768 | bytes 44717056 | tf_op jit(solution)/shard_map/dot_general | solution.py:61
  263.8 38.6 %all-reduce = (f32[256]{0:T(256)S(1)}, f32[1280]{0:T(1024)S(1)}) all-reduce(f32[256]{0:T(256)S(1)} %fusion.24, f32[1280]{0:T(1024)S(1)} %get-tuple-element.9), channel_id=1, replica_groups=mesh['batch'=16,'proto'=16] {'proto'}, use_global_device_ids=true, to_apply=%region_13.0 | all-reduce | flops 1536 | bytes 12288 | tf_op jit(solution)/shard_map/psum | solution.py:36
  302.4 3.5 fusion.20
  305.9 0.7 slice_bitcast_fusion.1
  306.7 7.8 %broadcast_in_dim.8 = f32[8,128,4096]{2,1,0:T(8,128)} broadcast(f32[128,4096]{1,0:T(8,128)S(1)} %get-tuple-element.11), dimensions={1,2} | broadcast | bytes 18874368 | tf_op jit(solution)/shard_map/broadcast_in_dim | solution.py:76
  314.6 16.9 %pad_maximum_fusion = f32[10,128,4096]{2,1,0:T(8,128)} fusion(f32[8,128,4096]{2,1,0:T(8,128)} %broadcast_in_dim.8, f32[1,128,4096]{2,1,0:T(8,128)S(1)} %get-tuple-element.12, f32[1,128,4096]{2,1,0:T(8,128)S(1)} %get-tuple-element.10), kind=kLoop, calls=%fused_computation.1 | loop fusion | flops 10485760 | bytes 41943040 | tf_op jit(solution)/shard_map/concatenate | solution.py:72
  331.5 1.4 slice-done.3
  332.9 1.2 slice-done.4
  334.1 16.6 %multiply_reduce_fusion = (f32[4096]{0:T(1024)S(1)}, f32[]{:T(128)}, bf16[1280,4096]{1,0:T(8,128)(2,1)}) fusion(f32[1280,4096]{1,0:T(8,128)S(1)} %bitcast.34, f32[1280]{0:T(1024)S(1)} %get-tuple-element.16, f32[10,128,4096]{2,1,0:T(8,128)} %pad_maximum_fusion, f32[1280]{0:T(1024)S(1)} %broadcast_bitcast_fusion), kind=kLoop, calls=%fused_computation.7 | loop fusion | flops 62910464 | bytes 52455428 | tf_op jit(solution)/shard_map/reduce_sum | solution.py:105
  350.7 8.0 %fusion.26 = f32[10,128,256]{2,1,0:T(8,128)} fusion(bf16[10,128,4096]{2,1,0:T(8,128)(2,1)} %bitcast.36, bf16[256,4096]{1,0:T(8,128)(2,1)S(1)} %copy-done.2, f32[4096]{0:T(1024)S(1)} %add_rsqrt_fusion), kind=kOutput, calls=%fused_computation.40 | convolution fusion | flops 2687500288 | bytes 13910016 | tf_op jit(solution)/shard_map/dot_general | solution.py:92
  358.8 18.1 %fusion.13 = f32[256,4096]{1,0:T(8,128)} fusion(bf16[10,128,256]{2,1,0:T(8,128)(2,1)S(1)} %get-tuple-element.14, f32[10,128,4096]{2,1,0:T(8,128)} %bitcast.35, f32[10,128]{1,0:T(8,128)S(1)} %get-tuple-element.15, f32[10]{0:T(128)S(1)} %compare_select_fusion, bf16[256,4096]{1,0:T(8,128)(2,1)} %param.6, f32[8,128,4096]{2,1,0:T(8,128)} %broadcast_in_dim.8, ...), kind=kOutput, calls=%fused_computation.27 | convolution fusion | flops 2725249024 | bytes 48927784 | tf_op jit(solution)/shard_map/dot_general | solution.py:107
  376.9 75.2 %psum.77 = f32[]{:T(128)} all-reduce(f32[]{:T(128)} %get-tuple-element.4), channel_id=1, replica_groups=mesh['batch'=16,'proto'=16] {'batch','proto'}, use_global_device_ids=true, to_apply=%region_19.20 | all-reduce | flops 1 | bytes 8 | tf_op jit(solution)/shard_map/psum | solution.py:86
  452.9 1.8 fusion.35
  454.7 118.7 %all-reduce.6.cloned.1.call-done = f32[256,4096]{1,0:T(8,128)} async-done(((f32[256,4096]{1,0:T(8,128)}), f32[256,4096]{1,0:T(8,128)}) %all-reduce.6.cloned.1.call-update) | async-done | bytes 4194320 | tf_op jit(solution)/shard_map/psum | solution.py:110
  573.4 1.7 dynamic-slice_multiply_fusion
  (36 shorter events, 0.4 us)
Async XLA Ops:
  7.2 445.7 %all-reduce.4.cloned.1.call-start = ((), (), s32[]{:S(2)}) async-start(), calls=%async_computation | async-start | bytes 2621440 | tf_op jit(solution)/shard_map/psum | solution.py:98
  193.9 52.4 %copy-start.3 = (bf16[10,128,256]{2,1,0:T(8,128)(2,1)S(1)}, bf16[10,128,256]{2,1,0:T(8,128)(2,1)}, u32[]{:S(2)}) copy-start(bf16[10,128,256]{2,1,0:T(8,128)(2,1)} %param.4) | copy-start | bytes 1966084
  197.1 50.8 %copy-start.1 = (bf16[256,4096]{1,0:T(8,128)(2,1)S(1)}, bf16[256,4096]{1,0:T(8,128)(2,1)}, u32[]{:S(2)}) copy-start(bf16[256,4096]{1,0:T(8,128)(2,1)} %param.6) | copy-start | bytes 6291460
  306.6 7.9 %copy-start = (f32[1,128,4096]{2,1,0:T(8,128)}, f32[1,128,4096]{2,1,0:T(8,128)S(1)}, u32[]{:S(2)}) copy-start(f32[1,128,4096]{2,1,0:T(8,128)S(1)} %get-tuple-element.12) | copy-start | bytes 6291460
  314.5 17.0 %slice-start = ((s8[20971520]{0:T(1024)(128)(4,1)}), s8[4194304]{0:T(1024)(128)(4,1)S(1)}, s32[]{:S(2)}) async-start(s8[20971520]{0:T(1024)(128)(4,1)} %bitcast.33), calls=%async_computation.2 | async-start | bytes 8388608
  314.5 17.0 %slice-start.1 = ((s8[20971520]{0:T(1024)(128)(4,1)}), s8[4194304]{0:T(1024)(128)(4,1)S(1)}, s32[]{:S(2)}) async-start(s8[20971520]{0:T(1024)(128)(4,1)} %bitcast.33), calls=%async_computation.3 | async-start | bytes 8388608
  314.5 17.0 %slice-start.2 = ((s8[20971520]{0:T(1024)(128)(4,1)}), s8[4194304]{0:T(1024)(128)(4,1)S(1)}, s32[]{:S(2)}) async-start(s8[20971520]{0:T(1024)(128)(4,1)} %bitcast.33), calls=%async_computation.4 | async-start | bytes 8388608
  314.6 18.4 %slice-start.3 = ((s8[20971520]{0:T(1024)(128)(4,1)}), s8[4194304]{0:T(1024)(128)(4,1)S(1)}, s32[]{:S(2)}) async-start(s8[20971520]{0:T(1024)(128)(4,1)} %bitcast.33), calls=%async_computation.5 | async-start | bytes 8388608
  314.6 19.6 %slice-start.4 = ((s8[20971520]{0:T(1024)(128)(4,1)}), s8[4194304]{0:T(1024)(128)(4,1)S(1)}, s32[]{:S(2)}) async-start(s8[20971520]{0:T(1024)(128)(4,1)} %bitcast.33), calls=%async_computation.6 | async-start | bytes 8388608
  334.1 16.6 %copy-start.2 = (bf16[256,4096]{1,0:T(8,128)(2,1)S(1)}, bf16[256,4096]{1,0:T(8,128)(2,1)}, u32[]{:S(2)}) copy-start(bf16[256,4096]{1,0:T(8,128)(2,1)} %param.6) | copy-start | bytes 6291460
  358.7 214.6 %all-reduce.6.cloned.1.call-start = ((), (), s32[]{:S(2)}) async-start(), calls=%async_computation.1 | async-start | bytes 8388608 | tf_op jit(solution)/shard_map/psum | solution.py:110
Sparse Core Ops, SparseCore 0:
  358.9 93.9 all-reduce.3
  455.3 118.0 all-reduce.5
where the time goes:
time: 587 us; the launch traced here: 583 us
  blocking collectives  329 us (56%)
  waiting for transfers between devices  119 us (20%)
  other arithmetic  62.5 us (11%)
  matrix products  46.1 us (8%)
  between operations  16 us (3%)
  local copies, waits for them, and re-layouts  10.6 us (2%)
    psum x3, blocking collectives, proto_step(): column_mass = lax.psum(jnp.sum(cluster_share, axis=0), 'batch')  139 us
    psum x1, waiting for transfers between devices, on_device(): term_total = lax.psum(product - unit_proto * curvature[None, :], 'batch')  119 us
    psum x3, blocking collectives, full_sweep(): row_mass = lax.psum(jnp.sum(cluster_share, axis=1), 'proto')  115 us
    psum x1, blocking collectives, on_device(): mean_loss = lax.psum(loss_part, ('batch', 'proto')) / (images_all * PAIRS)  75.2 us
    dot_general x1, matrix products, on_device(): lax.dot_general(student_bf, grad_cos, (((0,), (0,)), ((), ())), preferred...  18.1 us
    concatenate x1, other arithmetic, on_device(): jnp.concatenate([second_global[None], first_global[None], jnp.broadcast_t...  16.9 us
    reduce_sum x1, other arithmetic, on_device(): jnp.sum(logits * STUDENT_TEMP * grad_cos.astype(jnp.float32), axis=0)  16.6 us
    dot_general x1, matrix products, on_device(): jnp.dot(student_bf, proto_bf, preferred_element_type=jnp.float32)  15.4 us
  transfers between devices with their start and end apart: 2, of which 2 were waited for; matrix products, arithmetic and copies ran while one was open for 3% of the time, Pallas kernels for 0%

commit v1 on v0

v1 whole, which is shorter than its diff:
```python
import functools
import math

import jax
import jax.numpy as jnp
import numpy as np
from jax import lax
from jax.experimental import pallas as pl
from jax.experimental.pallas import tpu as pltpu
from jax.sharding import PartitionSpec as P

WIDE = 2
SK_ITERS = 3
PAIRS = 18
CORES = 2
STUDENT_TEMP = 0.1
TEACHER_TEMP = 0.07
NORM_EPS = 1e-06
MESH = pl.DeviceIdType.MESH
F32 = jnp.float32
BF16 = jnp.bfloat16
WIDTH = 512


def inverse_norm(squares):
    return lax.rsqrt(squares + NORM_EPS)


def kernel(
    nb,
    np_,
    sf_ref,
    tf_ref,
    sp_ref,
    tp_ref,
    loss_ref,
    gf_ref,
    gp_ref,
    share,
    expo,
    mixed,
    sraw,
    sbf,
    st,
    mix,
    pbf,
    pscale,
    racc,
    scale,
    grad,
    cot,
    cot_in,
    wt,
    wt_core,
    wt_ring,
    rowb,
    mass_out,
    mass_in,
    col_own,
    col,
    row_out,
    row_in,
    exp_out,
    exp_in,
    loss_cols,
    loss_out,
    loss_in,
    ex_send,
    ex_recv,
    core_send,
    core_recv,
    ring_send,
    ring_recv,
):
    b = lax.axis_index("batch")
    p = lax.axis_index("proto")
    nz = nb // CORES
    z, core = lax.div(b, CORES), lax.rem(b, CORES)
    columns = share.shape[1]
    crops, images, depth = sraw.shape
    rows = crops * images
    part = columns // nb
    steps = columns // WIDTH
    own = images // np_
    images_all = images * nb
    teacher_rows = WIDE * images_all
    clusters = columns * np_
    factor = 1.0 / (images_all * PAIRS * STUDENT_TEMP)
    trows = WIDE * images

    def batch_peer(k):
        return lax.rem(b + k, nb)

    def proto_peer(k):
        return lax.rem(p + k, np_)

    def over_batch(make):
        def body(k, carry):
            make(batch_peer(k)).start()
            return carry

        lax.fori_loop(1, nb, body, 0)

    def over_proto(make):
        def body(k, carry):
            make(proto_peer(k)).start()
            return carry

        lax.fori_loop(1, np_, body, 0)

    def await_all(block, n, sem):
        view = block.at[pl.ds(0, n - 1)]
        pltpu.make_async_copy(view, view, sem).wait()

    tfl = tf_ref[...].astype(F32)
    tbf = (tfl * inverse_norm(jnp.sum(tfl * tfl, axis=1, keepdims=True))).astype(BF16)

    barrier = pltpu.get_barrier_semaphore()

    def greet_batch(k, carry):
        pl.semaphore_signal(barrier, inc=1, device_id={"batch": batch_peer(k)}, device_id_type=MESH)
        return carry

    def greet_proto(k, carry):
        pl.semaphore_signal(barrier, inc=1, device_id={"proto": proto_peer(k)}, device_id_type=MESH)
        return carry

    lax.fori_loop(1, nb, greet_batch, 0)
    lax.fori_loop(1, np_, greet_proto, 0)

    def teacher_step(j, carry):
        at = pl.ds(pl.multiple_of(j * part, part), part)
        values = tp_ref[:, at].astype(F32)
        unit = (values * inverse_norm(jnp.sum(values * values, axis=0, keepdims=True))).astype(BF16)
        e = jnp.exp2(
            jnp.dot(tbf, unit, preferred_element_type=F32) * (math.log2(math.e) / TEACHER_TEMP)
        )
        share[:, at] = e
        mass_out[0, pl.ds(j, 1)] = jnp.sum(e, axis=0, keepdims=True)[None]
        return carry

    lax.fori_loop(0, nb, teacher_step, 0)
    pl.semaphore_wait(barrier, nb - 1 + np_ - 1)

    def send_mass(it):
        over_batch(
            lambda q: pltpu.make_async_remote_copy(
                mass_out.at[it, q],
                mass_in.at[it, b],
                ex_send.at[it],
                ex_recv.at[it],
                device_id={"batch": q},
                device_id_type=MESH,
            )
        )

    def send_columns(it):
        await_all(mass_in.at[it], nb, ex_recv.at[it])
        mass_in[it, pl.ds(b, 1)] = mass_out[it, pl.ds(b, 1)]
        total = jnp.sum(mass_in[it], axis=0, keepdims=True)
        factors = 1.0 / (clusters * total)
        col_own[it] = factors
        over_batch(
            lambda q: pltpu.make_async_remote_copy(
                col_own.at[it, 0],
                col.at[it, b],
                ex_send.at[3 + it],
                ex_recv.at[3 + it],
                device_id={"batch": q},
                device_id_type=MESH,
            )
        )

    def send_rows(it):
        await_all(col.at[it], nb, ex_recv.at[3 + it])
        col[it, pl.ds(b, 1)] = col_own[it]

        def body(j, acc):
            at = pl.ds(pl.multiple_of(j * part, part), part)
            weighted = share[:, at] * col[it, j]
            if it == SK_ITERS - 1:
                share[:, at] = weighted
            for lane in range(0, part, 128):
                acc = acc + weighted[:, lane : lane + 128]
            return acc

        acc = lax.fori_loop(0, nb, body, jnp.zeros((trows, 128), F32))
        row_out[it] = jnp.sum(acc.T, axis=0, keepdims=True)
        over_proto(
            lambda q: pltpu.make_async_remote_copy(
                row_out.at[it],
                row_in.at[it, p],
                ex_send.at[6 + it],
                ex_recv.at[6 + it],
                device_id={"proto": q},
                device_id_type=MESH,
            )
        )

    def row_factors(it):
        await_all(row_in.at[it], np_, ex_recv.at[6 + it])
        row_in[it, pl.ds(p, 1)] = row_out[it][None]
        return 1.0 / jnp.sum(row_in[it], axis=0)

    def mass_of_rows(it, inverse):
        rowb[...] = jnp.broadcast_to(inverse * (1.0 / teacher_rows), (128, trows)).T

        def body(j, carry):
            for lane in range(0, part, 128):
                at = pl.ds(pl.multiple_of(j * part + lane, 128), 128)
                mass_out[it, j, :, lane : lane + 128] = jnp.sum(
                    share[:, at] * rowb[...], axis=0, keepdims=True
                )
            return carry

        lax.fori_loop(0, nb, body, 0)

    def student_rows():
        def body(c, carry):
            first, second = carry
            at = pl.ds(pl.multiple_of(c * images, images), images)
            values = sf_ref[at, :].astype(F32)
            sraw[c] = values
            unit = (values * inverse_norm(jnp.sum(values * values, axis=1, keepdims=True))).astype(BF16)
            sbf[at, :] = unit
            wide = unit.astype(F32)
            st[:, at] = wide.T.astype(BF16)
            first = first + jnp.where(c == 0, 0.0, 1.0) * wide
            second = second + jnp.where(c == 1, 0.0, 1.0) * wide
            return first, second

        zero = jnp.zeros((images, depth), F32)
        sums = lax.fori_loop(0, crops, body, (zero, zero))
        for i, values in enumerate(sums):
            high = values.astype(BF16)
            mix[i * images : (i + 1) * images, :] = high
            mix[trows + i * images : trows + (i + 1) * images, :] = (values - high.astype(F32)).astype(BF16)
        racc[...] = jnp.zeros_like(racc)

    def student_prototypes():
        def body(j, carry):
            at = pl.ds(pl.multiple_of(j * part, part), part)
            values = sp_ref[:, at].astype(F32)
            inverse = inverse_norm(jnp.sum(values * values, axis=0, keepdims=True))
            pscale[:, at] = inverse
            pbf[:, at] = (values * inverse).astype(BF16)
            return carry

        lax.fori_loop(0, nb, body, 0)

    def student_steps(low, high):
        def body(j, carry):
            at = pl.ds(pl.multiple_of(j * WIDTH, WIDTH), WIDTH)
            block = pbf[:, at]
            e = jnp.exp2(
                jnp.dot(sbf[...], block, preferred_element_type=F32) * (math.log2(math.e) / STUDENT_TEMP)
            )
            expo[:, at] = e
            acc = racc[...]
            for lane in range(0, WIDTH, 128):
                acc = acc + e[:, lane : lane + 128]
            racc[...] = acc
            both = jnp.dot(mix[...], block, preferred_element_type=F32)
            mixed[:, at] = (both[:trows] + both[trows:]) * (1.0 / STUDENT_TEMP)
            return carry

        lax.fori_loop(low, high, body, 0)

    def send_exponentials():
        for c in range(crops):
            exp_out[c] = jnp.sum(racc[c * images : (c + 1) * images, :].T, axis=0, keepdims=True)
        over_proto(
            lambda q: pltpu.make_async_remote_copy(
                exp_out,
                exp_in.at[p],
                ex_send.at[9],
                ex_recv.at[9],
                device_id={"proto": q},
                device_id_type=MESH,
            )
        )

    def student_scales():
        await_all(exp_in, np_, ex_recv.at[9])
        exp_in[pl.ds(p, 1)] = exp_out[...][None]
        for c in range(crops):
            total = jnp.sum(exp_in[:, c], axis=0)
            pairs = 1.0 if c < 2 else 2.0
            scale[c * images : (c + 1) * images, :] = jnp.broadcast_to(
                (pairs * factor) / total, (128, images)
            ).T

    cut = [0, steps // 4, steps // 2, 3 * steps // 4, steps]
    send_mass(0)
    student_rows()
    send_columns(0)
    student_prototypes()
    send_rows(0)
    student_steps(cut[0], cut[1])
    mass_of_rows(1, row_factors(0))
    send_mass(1)
    student_steps(cut[1], cut[2])
    send_columns(1)
    student_steps(cut[2], cut[3])
    send_rows(1)
    student_steps(cut[3], cut[4])
    mass_of_rows(2, row_factors(1))
    send_mass(2)
    send_exponentials()
    send_columns(2)
    loss_cols[...] = jnp.zeros_like(loss_cols)
    cot[...] = jnp.zeros_like(cot)
    student_scales()
    send_rows(2)
    last = row_factors(2)
    rowb[...] = jnp.broadcast_to(last * factor, (128, trows)).T

    def core_copy(t):
        return pltpu.make_async_remote_copy(
            wt.at[t, :, 1 - core],
            wt_core.at[t],
            core_send.at[t],
            core_recv.at[t],
            device_id={"batch": z * CORES + 1 - core},
            device_id_type=MESH,
        )

    def ring_copy(t, s):
        way = 1 - 2 * lax.rem(t, 2)
        segment = lax.rem(z - way * (1 + s) + 2 * nz, nz)
        to = lax.rem(z + way + nz, nz)
        return pltpu.make_async_remote_copy(
            wt.at[t, segment, core],
            wt_ring.at[t, s],
            ring_send.at[t, s],
            ring_recv.at[t, s],
            device_id={"batch": to * CORES + core},
            device_id_type=MESH,
        )

    def serve(t, phase):
        @pl.when(phase == 1)
        def _():
            core_copy(t).wait_recv()
            for segment in range(nz):
                wt[t, segment, pl.ds(core, 1)] += wt_core[t, pl.ds(segment, 1)]
            ring_copy(t, 0).start()

        @pl.when(jnp.logical_and(phase >= 2, phase <= nz))
        def _():
            s = phase - 2
            way = 1 - 2 * lax.rem(t, 2)
            segment = lax.rem(z - way * (2 + s) + 2 * nz, nz)
            ring_copy(t, s).wait_recv()
            wt[t, segment, core] += wt_ring[t, s]

            @pl.when(s < nz - 2)
            def _():
                ring_copy(t, s + 1).start()

            @pl.when(s == nz - 2)
            def _():
                at = pl.ds(pl.multiple_of(t * WIDTH, WIDTH), WIDTH)
                gp_ref[:, at] = pscale[:, at] * wt[t, z, core]

    def serve_all(k):
        def body(t, carry):
            serve(t, k - t)
            return carry

        lax.fori_loop(0, jnp.minimum(k, steps), body, 0)

    def gradient_step(j, carry):
        at = pl.ds(pl.multiple_of(j * WIDTH, WIDTH), WIDTH)
        loss_acc = loss_cols[...]
        row0 = jnp.concatenate([rowb[:images, :]] * (WIDTH // 128), axis=1)
        row1 = jnp.concatenate([rowb[images:, :]] * (WIDTH // 128), axis=1)
        first = share[:images, at] * row0
        second = share[images:, at] * row1
        loss_acc = loss_acc + jnp.sum(first * mixed[:images, at], axis=0, keepdims=True)
        loss_acc = loss_acc + jnp.sum(second * mixed[images:, at], axis=0, keepdims=True)
        loss_cols[...] = loss_acc
        both = first + second
        for c in range(crops):
            own_rows = slice(c * images, (c + 1) * images)
            target = second if c == 0 else first if c == 1 else both
            scales = jnp.concatenate([scale[own_rows, :]] * (WIDTH // 128), axis=1)
            grad[own_rows, :] = (expo[own_rows, at] * scales - target).astype(BF16)
        block = pbf[:, at]
        g = grad[...]
        product = jnp.dot(st[...], g, preferred_element_type=F32)
        inverse = pscale[:, at]
        unit = sp_ref[:, at].astype(F32) * inverse
        curvature = jnp.sum(block.astype(F32) * product, axis=0, keepdims=True)
        wt[j] = (product - unit * curvature).reshape(wt.shape[1:])
        core_copy(j).start()
        cot[...] += lax.dot_general(g, block, (((1,), (1,)), ((), ())), preferred_element_type=F32).reshape(
            cot.shape
        )
        serve_all(j)
        return carry

    lax.fori_loop(0, steps, gradient_step, 0)

    over_proto(
        lambda q: pltpu.make_async_remote_copy(
            cot.at[:, pl.ds(pl.multiple_of(q * own, own), own)],
            cot_in.at[p],
            ex_send.at[12],
            ex_recv.at[12],
            device_id={"proto": q},
            device_id_type=MESH,
        )
    )

    portion = row_out[SK_ITERS - 1] * last
    logs = [jnp.log(jnp.sum(exp_in[:, c], axis=0)) for c in range(crops)]
    shared = functools.reduce(lambda x, y: x + y, logs[2:])
    lossv = portion[:, :images] * (logs[1] + shared) + portion[:, images:] * (logs[0] + shared)
    for lane in range(0, WIDTH, 128):
        lossv = lossv - loss_cols[:, lane : lane + 128] * (1.0 / factor)
    loss_out[0] = lossv
    over_proto(
        lambda q: pltpu.make_async_remote_copy(
            loss_out.at[0],
            loss_in.at[0, p],
            ex_send.at[10],
            ex_recv.at[10],
            device_id={"proto": q},
            device_id_type=MESH,
        )
    )

    def tail(k, carry):
        serve_all(k)
        return carry

    lax.fori_loop(steps, steps + 2, tail, 0)
    await_all(loss_in.at[0], np_, ex_recv.at[10])
    loss_in[0, pl.ds(p, 1)] = loss_out[0][None]
    loss_out[1] = jnp.sum(loss_in[0, :np_], axis=0)
    over_batch(
        lambda q: pltpu.make_async_remote_copy(
            loss_out.at[1],
            loss_in.at[1, b],
            ex_send.at[11],
            ex_recv.at[11],
            device_id={"batch": q},
            device_id_type=MESH,
        )
    )
    lax.fori_loop(steps + 2, steps + nz + 1, tail, 0)

    await_all(loss_in.at[1], nb, ex_recv.at[11])
    loss_in[1, pl.ds(b, 1)] = loss_out[1][None]
    total = jnp.sum(loss_in[1, :nb], axis=0)
    loss_ref[...] = jnp.sum(total, axis=1, keepdims=True) * (1.0 / (images_all * PAIRS))

    await_all(cot_in, np_, ex_recv.at[12])
    mine = pl.ds(pl.multiple_of(p * own, own), own)
    cot_in[pl.ds(p, 1)] = cot[:, mine][None]
    total = jnp.sum(cot_in[...], axis=0)
    values = sraw[:, mine]
    inverse = inverse_norm(jnp.sum(values * values, axis=2, keepdims=True))
    unit = values * inverse
    gf_ref[...] = inverse * (total - unit * jnp.sum(unit * total, axis=2, keepdims=True))

    for it in range(SK_ITERS):
        await_all(mass_out.at[it], nb, ex_send.at[it])
        await_all(col.at[it], nb, ex_send.at[3 + it])
        await_all(row_in.at[it], np_, ex_send.at[6 + it])
    await_all(exp_in, np_, ex_send.at[9])
    await_all(loss_in.at[0], np_, ex_send.at[10])
    await_all(loss_in.at[1], nb, ex_send.at[11])
    await_all(cot_in, np_, ex_send.at[12])

    def sent(t, carry):
        core_copy(t).wait_send()

        def one(s, c):
            ring_copy(t, s).wait_send()
            return c

        lax.fori_loop(0, nz - 1, one, 0)
        return carry

    lax.fori_loop(0, steps, sent, 0)


def on_device(student_features, teacher_features, student_prototypes, teacher_prototypes):
    crops, images, depth = student_features.shape
    columns = student_prototypes.shape[1]
    nb, np_ = lax.axis_size("batch"), lax.axis_size("proto")
    nz = nb // CORES
    rows, trows = crops * images, WIDE * images
    steps, part, deep = columns // WIDTH, columns // nb, depth // nb
    vmem = pltpu.VMEM
    dma = pltpu.SemaphoreType.DMA
    loss, grad_features, grad_prototypes = pl.pallas_call(
        functools.partial(kernel, nb, np_),
        out_shape=(
            jax.ShapeDtypeStruct((1, 1), F32),
            jax.ShapeDtypeStruct((crops, images // np_, depth), F32),
            jax.ShapeDtypeStruct((deep, columns), F32),
        ),
        in_specs=[pl.BlockSpec(memory_space=vmem)] * 4,
        out_specs=[pl.BlockSpec(memory_space=vmem)] * 3,
        scratch_shapes=[
            vmem((trows, columns), F32),
            vmem((rows, columns), F32),
            vmem((trows, columns), F32),
            vmem((crops, images, depth), F32),
            vmem((rows, depth), BF16),
            vmem((depth, rows), BF16),
            vmem((2 * trows, depth), BF16),
            vmem((depth, columns), BF16),
            vmem((1, columns), F32),
            vmem((rows, 128), F32),
            vmem((rows, 128), F32),
            vmem((rows, WIDTH), BF16),
            vmem((crops, images, depth), F32),
            vmem((np_, crops, images // np_, depth), F32),
            vmem((steps, nz, CORES, deep, WIDTH), F32),
            vmem((steps, nz, deep, WIDTH), F32),
            vmem((steps, nz - 1, deep, WIDTH), F32),
            vmem((trows, 128), F32),
            vmem((SK_ITERS, nb, 1, part), F32),
            vmem((SK_ITERS, nb, 1, part), F32),
            vmem((SK_ITERS, 1, 1, part), F32),
            vmem((SK_ITERS, nb, 1, part), F32),
            vmem((SK_ITERS, 1, trows), F32),
            vmem((SK_ITERS, np_, 1, trows), F32),
            vmem((crops, 1, images), F32),
            vmem((np_, crops, 1, images), F32),
            vmem((1, WIDTH), F32),
            vmem((2, 1, 128), F32),
            vmem((2, max(nb, np_), 1, 128), F32),
            dma((13,)),
            dma((13,)),
            dma((steps,)),
            dma((steps,)),
            dma((steps, nz - 1)),
            dma((steps, nz - 1)),
        ],
        compiler_params=pltpu.CompilerParams(
            collective_id=0, has_side_effects=True, vmem_limit_bytes=62 * 1024 * 1024
        ),
    )(
        student_features.reshape(rows, depth),
        teacher_features.reshape(trows, depth),
        student_prototypes,
        teacher_prototypes,
    )
    return loss[0, 0], grad_features, grad_prototypes


def solution(mesh):
    return jax.shard_map(
        on_device,
        mesh=mesh,
        in_specs=(P(None, "batch", None), P(None, "batch", None), P(None, "proto"), P(None, "proto")),
        out_specs=(P(), P(None, ("batch", "proto"), None), P("batch", "proto")),
        check_vma=False,
    )
```

time: 587 us -> 122 us (0.21)
  blocking collectives: 329 us -> 0 us
  waiting for transfers between devices: 119 us -> 0 us
  Pallas kernels: 0 us -> 116 us
  other arithmetic: 62.5 us -> 0 us
  matrix products: 46.1 us -> 0 us
  between operations: 16 us -> 2.39 us
  local copies, waits for them, and re-layouts: 10.6 us -> 3.2 us
    psum x7 -> x0, blocking collectives: 329 us -> none  [the longest x3 139 us: proto_step(): column_mass = lax.psum(jnp.sum(cluster_share, axis=0), 'batch')]
    psum x2 -> x0, waiting for transfers between devices: 119 us -> none  [the longest x1 119 us: on_device(): term_total = lax.psum(product - unit_proto * curvature[None, :], 'batch')]
    pallas_call x0 -> x1, Pallas kernels: none -> 116 us  [on_device(): pl.pallas_call(functools.partial(kernel, nb, np_), out_shape=(jax.ShapeDt...]
    dot_general x4 -> x0, matrix products: 46.1 us -> none  [the longest x1 18.1 us: on_device(): lax.dot_general(student_bf, grad_cos, (((0,), (0,)), ((), ())), preferred...]
    reduce_sum x10 -> x0, other arithmetic: 35.5 us -> none  [the longest x1 16.6 us: on_device(): jnp.sum(logits * STUDENT_TEMP * grad_cos.astype(jnp.float32), axis=0)]
    concatenate x1 -> x0, other arithmetic: 16.9 us -> none  [on_device(): jnp.concatenate([second_global[None], first_global[None], jnp.broadcast_t...]
    mul x10 -> x0, other arithmetic: 8.31 us -> none  [the longest x1 3.49 us: on_device(): teacher_rows * cluster_share]
    broadcast_in_dim x1 -> x0, local copies, waits for them, and re-layouts: 7.81 us -> none  [on_device(): jnp.broadcast_to(summed[None], (crop_count - 2, img_local, proto_local))]
  transfers between devices with their start and end apart: 2 -> 0, of which waited for: 2 -> 0; matrix products, arithmetic and copies ran while one was open for 3% -> 0% of each run, Pallas kernels for 0% -> 0%
where the time goes in v1:
time: 122 us
  Pallas kernels  116 us (95%)
  local copies, waits for them, and re-layouts  3.2 us (3%)
  between operations  2.39 us (2%)
    pallas_call x1, Pallas kernels, on_device(): pl.pallas_call(functools.partial(kernel, nb, np_), out_shape=(jax.ShapeDt...  116 us
    unnamed x2, local copies, waits for them, and re-layouts  3.2 us

profile of v1, /device:TPU:32, one launch (start us, length us, event | category | flops | bytes accessed | tf_op | source)
XLA Modules:
  0.0 122.0 jit_solution(11501215305233024064)
XLA Ops:
  0.6 116.4 %shard_map.67 = (f32[1,1]{1,0:T(1,128)}, f32[10,8,256]{2,1,0:T(8,128)}, f32[16,4096]{1,0:T(8,128)}) custom-call(bf16[1280,256]{1,0:T(8,128)(2,1)} %bitcast.3, bf16[256,256]{1,0:T(8,128)(2,1)} %bitcast.4, bf16[256,4096]{1,0:T(8,128)(2,1)} %sp_ref.1, bf16[256,4096]{1,0:T(8,128)(2,1)} %tp_ref.1), custom_call_target="tpu_custom_call" | custom-call | tf_op jit(solution)/shard_map/pallas_call | solution.py:499
  117.7 1.5 %copy.11 = f32[10,8,256]{2,1,0:T(8,128)} copy(f32[10,8,256]{2,1,0:T(8,128)} %get-tuple-element.13) | data formatting | bytes 163840
  119.2 1.7 %copy.12 = f32[16,4096]{1,0:T(8,128)} copy(f32[16,4096]{1,0:T(8,128)} %get-tuple-element.14) | data formatting | bytes 524288

commit v2 on v1

v2 whole, which is shorter than its diff:
```python
import functools
import math

import jax
import jax.numpy as jnp
from jax import lax
from jax.experimental import pallas as pl
from jax.experimental.pallas import tpu as pltpu
from jax.sharding import PartitionSpec as P

WIDE = 2
SK_ITERS = 3
PAIRS = 18
CORES = 2
STUDENT_TEMP = 0.1
TEACHER_TEMP = 0.07
NORM_EPS = 1e-06
MESH = pl.DeviceIdType.MESH
F32 = jnp.float32
BF16 = jnp.bfloat16
WIDTH = 512
PART = 256
LAG = 4
GROUPS = 2


def inverse_norm(squares):
    return lax.rsqrt(squares + NORM_EPS)


def kernel(
    nb,
    np_,
    sf_hbm,
    tf_hbm,
    sp_hbm,
    tp_hbm,
    loss_ref,
    gf_ref,
    gp_ref,
    sf_ref,
    tf_ref,
    sp_ref,
    pbf,
    tbf,
    tsend,
    trecv,
    share,
    expo,
    mixed,
    sraw,
    sbf,
    st,
    mix,
    pscale,
    racc,
    scale,
    grad,
    cot,
    cot_in,
    wt,
    wt_core,
    wt_ring,
    rowb,
    mass_out,
    mass_in,
    col,
    row_out,
    row_in,
    row_inv,
    exp_out,
    exp_in,
    loss_cols,
    loss_out,
    loss_plane,
    loss_z,
    load_sem,
    ex_send,
    ex_recv,
    cot_send,
    cot_recv,
    core_send,
    core_recv,
    ring_send,
    ring_recv,
):
    b = lax.axis_index("batch")
    p = lax.axis_index("proto")
    nz = nb // CORES
    z, core = lax.div(b, CORES), lax.rem(b, CORES)
    other = 1 - core
    half = share.shape[2]
    lanes = half // 128
    columns = CORES * half
    crops, images, depth = sraw.shape
    steps = columns // WIDTH
    own = images // np_
    images_all = images * nb
    teacher_rows = WIDE * images_all
    clusters = columns * np_
    factor = 1.0 / (images_all * PAIRS * STUDENT_TEMP)
    trows = WIDE * images
    plane = CORES * np_
    here = core * np_ + p
    hops = (nz // 2, nz - 1 - nz // 2)

    z_peers = [{"batch": lax.rem(z + k, nz) * CORES + core} for k in range(1, nz)]
    proto_peers = [lax.rem(p + k, np_) for k in range(1, np_)]
    plane_peers = [{"proto": q} for q in proto_peers]
    plane_peers += [{"batch": z * CORES + other, "proto": q} for q in proto_peers]
    plane_peers += [{"batch": z * CORES + other}]

    def send(peers, source, target, sends, receives):
        for peer in peers:
            pltpu.make_async_remote_copy(
                source, target, sends, receives, device_id=peer, device_id_type=MESH
            ).start()

    def await_all(block, n, sem):
        view = block.at[pl.ds(0, n - 1)]
        pltpu.make_async_copy(view, view, sem).wait()

    def half_of(ref, which):
        return ref.at[:, pl.ds(pl.multiple_of(which * half, half), half)]

    loads = [
        pltpu.make_async_copy(tf_hbm, tf_ref, load_sem.at[0]),
        pltpu.make_async_copy(half_of(tp_hbm, core), half_of(pbf, core), load_sem.at[1]),
        pltpu.make_async_copy(half_of(tp_hbm, other), half_of(pbf, other), load_sem.at[2]),
        pltpu.make_async_copy(sf_hbm, sf_ref, load_sem.at[3]),
        pltpu.make_async_copy(sp_hbm, sp_ref, load_sem.at[4]),
    ]
    barrier = pltpu.get_barrier_semaphore()
    for peer in z_peers + plane_peers:
        pl.semaphore_signal(barrier, inc=1, device_id=peer, device_id_type=MESH)
    for load in loads:
        load.start()

    loads[0].wait()
    values = tf_ref[...].astype(F32)
    unit = (values * inverse_norm(jnp.sum(values * values, axis=1, keepdims=True))).astype(BF16)
    tbf[0] = unit
    tsend[...] = unit.astype(F32)

    def teacher_unit(which, j):
        at = pl.ds(pl.multiple_of(which * half + j * PART, PART), PART)
        values = pbf[:, at].astype(F32)
        return at, (values * inverse_norm(jnp.sum(values * values, axis=0, keepdims=True))).astype(BF16)

    def teacher_exp(rows, unit):
        logits = jnp.dot(tbf[rows], unit, preferred_element_type=F32)
        return jnp.exp2(logits * (math.log2(math.e) / TEACHER_TEMP))

    def own_half(j, carry):
        at, unit = teacher_unit(core, j)
        pbf[:, at] = unit
        share[core, :, pl.ds(pl.multiple_of(j * PART, PART), PART)] = teacher_exp(0, unit)
        return carry

    def far_half(j, carry):
        at, unit = teacher_unit(other, j)
        share[other, :, pl.ds(pl.multiple_of(j * PART, PART), PART)] = teacher_exp(0, unit)
        return carry

    def other_rows(j, carry):
        at = pl.ds(pl.multiple_of(j * PART, PART), PART)
        e = teacher_exp(1, pbf[:, pl.ds(pl.multiple_of(core * half + j * PART, PART), PART)])
        share[2, :, at] = e
        mass = jnp.sum(share[core, :, at], axis=0, keepdims=True) + jnp.sum(e, axis=0, keepdims=True)
        for lane in range(PART // 128):
            mass_out[0, pl.ds(j * (PART // 128) + lane, 1)] = mass[:, lane * 128 : (lane + 1) * 128]
        return carry

    loads[1].wait()
    lax.fori_loop(0, half // PART // 2, own_half, 0)
    pl.semaphore_wait(barrier, nz - 1 + plane - 1)
    teacher_copy = pltpu.make_async_remote_copy(
        tsend,
        trecv,
        ex_send.at[9],
        ex_recv.at[9],
        device_id={"batch": z * CORES + other},
        device_id_type=MESH,
    )
    teacher_copy.start()
    lax.fori_loop(half // PART // 2, half // PART, own_half, 0)
    teacher_copy.wait_recv()
    tbf[1] = trecv[...].astype(BF16)
    lax.fori_loop(0, half // PART, other_rows, 0)

    def send_mass(it):
        send(z_peers, mass_out.at[it], mass_in.at[it, z], ex_send.at[it], ex_recv.at[it])

    def send_rows(it):
        await_all(mass_in.at[it], nz, ex_recv.at[it])
        mass_in[it, pl.ds(z, 1)] = mass_out[it][None]
        col[it, core] = 1.0 / (clusters * jnp.sum(mass_in[it], axis=0))
        for which, block in ((core, core), (2, other)):

            def body(j, acc):
                at = pl.ds(pl.multiple_of(j * 128, 128), 128)
                return acc + share[which, :, at] * col[it, core, pl.ds(j, 1)]

            acc = lax.fori_loop(0, lanes, body, jnp.zeros((trows, 128), F32), unroll=4)
            for crop in range(WIDE):
                row_out[it, pl.ds(block * WIDE + crop, 1)] = jnp.sum(
                    acc[crop * images : (crop + 1) * images].T, axis=0, keepdims=True
                )
        send(plane_peers, row_out.at[it], row_in.at[it, here], ex_send.at[3 + it], ex_recv.at[3 + it])

    def row_factors(it, numerator, both):
        await_all(row_in.at[it], plane, ex_recv.at[3 + it])
        row_in[it, pl.ds(here, 1)] = row_out[it][None]
        row_inv[...] = 1.0 / jnp.sum(row_in[it], axis=0)
        for side, block in ((0, core), (1, other))[: 2 if both else 1]:
            for crop in range(WIDE):
                line = row_inv[pl.ds(block * WIDE + crop, 1)] * numerator
                rowb[side, crop * images : (crop + 1) * images] = jnp.broadcast_to(line, (128, images)).T

    def mass_of_rows(it):
        def body(j, carry):
            at = pl.ds(pl.multiple_of(j * 128, 128), 128)
            product = share[core, :, at] * rowb[0] + share[2, :, at] * rowb[1]
            mass_out[it, pl.ds(j, 1)] = jnp.sum(product, axis=0, keepdims=True)
            return carry

        lax.fori_loop(0, lanes, body, 0, unroll=2)

    def student_rows():
        loads[3].wait()

        def body(c, carry):
            first, second = carry
            at = pl.ds(pl.multiple_of(c * images, images), images)
            values = sf_ref[at, :].astype(F32)
            sraw[c] = values
            unit = (values * inverse_norm(jnp.sum(values * values, axis=1, keepdims=True))).astype(BF16)
            sbf[at, :] = unit
            wide = unit.astype(F32)
            st[:, at] = wide.T.astype(BF16)
            first = first + jnp.where(c == 0, 0.0, 1.0) * wide
            second = second + jnp.where(c == 1, 0.0, 1.0) * wide
            return first, second

        zero = jnp.zeros((images, depth), F32)
        sums = lax.fori_loop(0, crops, body, (zero, zero))
        for i, values in enumerate(sums):
            high = values.astype(BF16)
            mix[i * images : (i + 1) * images, :] = high
            mix[trows + i * images : trows + (i + 1) * images, :] = (values - high.astype(F32)).astype(BF16)
        racc[...] = jnp.zeros_like(racc)

    def student_prototypes():
        loads[4].wait()

        def body(j, carry):
            at = pl.ds(pl.multiple_of(j * PART, PART), PART)
            values = sp_ref[:, at].astype(F32)
            inverse = inverse_norm(jnp.sum(values * values, axis=0, keepdims=True))
            pscale[:, at] = inverse
            pbf[:, at] = (values * inverse).astype(BF16)
            return carry

        lax.fori_loop(0, columns // PART, body, 0)

    def student_steps(low, high):
        def body(j, carry):
            at = pl.ds(pl.multiple_of(j * WIDTH, WIDTH), WIDTH)
            block = pbf[:, at]
            e = jnp.exp2(
                jnp.dot(sbf[...], block, preferred_element_type=F32) * (math.log2(math.e) / STUDENT_TEMP)
            )
            expo[:, at] = e
            acc = racc[...]
            for lane in range(0, WIDTH, 128):
                acc = acc + e[:, lane : lane + 128]
            racc[...] = acc
            both = jnp.dot(mix[...], block, preferred_element_type=F32)
            mixed[:, at] = (both[:trows] + both[trows:]) * (1.0 / STUDENT_TEMP)
            return carry

        lax.fori_loop(low, high, body, 0)

    def send_exponentials():
        for c in range(crops):
            exp_out[c] = jnp.sum(racc[c * images : (c + 1) * images, :].T, axis=0, keepdims=True)
        send(plane_peers[: np_ - 1], exp_out, exp_in.at[p], ex_send.at[6], ex_recv.at[6])

    def student_scales():
        await_all(exp_in, np_, ex_recv.at[6])
        exp_in[pl.ds(p, 1)] = exp_out[...][None]
        for c in range(crops):
            total = jnp.sum(exp_in[:, c], axis=0)
            pairs = 1.0 if c < 2 else 2.0
            scale[c * images : (c + 1) * images, :] = jnp.broadcast_to(
                (pairs * factor) / total, (128, images)
            ).T

    send_mass(0)
    loads[2].wait()
    lax.fori_loop(0, half // PART, far_half, 0)
    student_rows()
    send_rows(0)
    student_prototypes()
    student_steps(0, steps // 8)
    row_factors(0, 1.0 / teacher_rows, True)
    mass_of_rows(1)
    send_mass(1)
    student_steps(steps // 8, steps // 2)
    send_rows(1)
    student_steps(steps // 2, steps)
    row_factors(1, 1.0 / teacher_rows, True)
    mass_of_rows(2)
    send_mass(2)
    send_exponentials()
    loss_cols[...] = jnp.zeros_like(loss_cols)
    send_rows(2)
    column_copy = pltpu.make_async_remote_copy(
        col.at[2, core],
        col.at[2, core],
        ex_send.at[10],
        ex_recv.at[10],
        device_id={"batch": z * CORES + other},
        device_id_type=MESH,
    )
    column_copy.start()
    student_scales()
    column_copy.wait_recv()

    def weigh(j, carry):
        at = pl.ds(pl.multiple_of(j * 128, 128), 128)
        for h in range(CORES):
            share[h, :, at] = share[h, :, at] * col[2, h, pl.ds(j, 1)]
        return carry

    lax.fori_loop(0, lanes, weigh, 0)
    row_factors(2, factor, False)

    def core_copy(t):
        return pltpu.make_async_remote_copy(
            wt.at[t, :, other],
            wt_core.at[t],
            core_send.at[t],
            core_recv.at[t],
            device_id={"batch": z * CORES + other},
            device_id_type=MESH,
        )

    def way_of(t, side):
        way = 1 - 2 * lax.rem(t, 2)
        return -way if side else way

    def ring_copy(t, side, s):
        way = way_of(t, side)
        segment = lax.rem(z + way * (hops[side] - s) + nz, nz)
        return pltpu.make_async_remote_copy(
            wt.at[t, segment, core],
            wt_ring.at[t, side, s],
            ring_send.at[t, side, s],
            ring_recv.at[t, side, s],
            device_id={"batch": lax.rem(z + way + nz, nz) * CORES + core},
            device_id_type=MESH,
        )

    def serve(t, phase):
        if phase == 0:
            core_copy(t).wait_recv()
            for segment in range(nz):
                wt[t, segment, pl.ds(core, 1)] += wt_core[t, pl.ds(segment, 1)]
            for side in range(2):
                if hops[side]:
                    ring_copy(t, side, 0).start()
            return
        s = phase - 1
        for side in range(2):
            if s < hops[side]:
                segment = lax.rem(z + way_of(t, side) * (hops[side] - 1 - s) + nz, nz)
                ring_copy(t, side, s).wait_recv()
                wt[t, segment, core] += wt_ring[t, side, s]
                if s + 1 < hops[side]:
                    ring_copy(t, side, s + 1).start()
        if s + 1 == hops[0]:
            at = pl.ds(pl.multiple_of(t * WIDTH, WIDTH), WIDTH)
            gp_ref[:, at] = pscale[:, at] * wt[t, z, core]

    def serve_all(k):
        for phase in range(hops[0], -1, -1):
            t = k - 1 - LAG * phase

            @pl.when(jnp.logical_and(t >= 0, t < steps))
            def _():
                serve(t, phase)

    def gradient_step(j, carry):
        at = pl.ds(pl.multiple_of(j * WIDTH, WIDTH), WIDTH)
        which = lax.div(j, steps // CORES)
        inside = pl.ds(pl.multiple_of((j - which * (steps // CORES)) * WIDTH, WIDTH), WIDTH)
        row0 = jnp.concatenate([rowb[0, :images, :]] * (WIDTH // 128), axis=1)
        row1 = jnp.concatenate([rowb[0, images:, :]] * (WIDTH // 128), axis=1)
        first = share[which, :images, inside] * row0
        second = share[which, images:, inside] * row1
        loss_cols[...] += jnp.sum(
            first * mixed[:images, at] + second * mixed[images:, at], axis=0, keepdims=True
        )
        both = first + second
        for c in range(crops):
            own_rows = slice(c * images, (c + 1) * images)
            target = second if c == 0 else first if c == 1 else both
            scales = jnp.concatenate([scale[own_rows, :]] * (WIDTH // 128), axis=1)
            grad[own_rows, at] = (expo[own_rows, at] * scales - target).astype(BF16)
        product = jnp.dot(st[...], grad[:, at], preferred_element_type=F32)
        unit = sp_ref[:, at].astype(F32) * pscale[:, at]
        curvature = jnp.sum(pbf[:, at].astype(F32) * product, axis=0, keepdims=True)
        wt[j] = (product - unit * curvature).reshape(wt.shape[1:])
        core_copy(j).start()
        serve_all(j)
        return carry

    lax.fori_loop(0, steps, gradient_step, 0)

    size = crops // GROUPS
    for group in range(GROUPS):
        low = group * size
        cot[low : low + size] = lax.dot_general(
            grad[low * images : (low + size) * images, :],
            pbf[...],
            (((1,), (1,)), ((), ())),
            preferred_element_type=F32,
        ).reshape(size, images, depth)
        for q in proto_peers:
            pltpu.make_async_remote_copy(
                cot.at[low : low + size, pl.ds(pl.multiple_of(q * own, own), own)],
                cot_in.at[group, p],
                cot_send.at[group],
                cot_recv.at[group],
                device_id={"proto": q},
                device_id_type=MESH,
            ).start()
        serve_all(steps + group)

    inverse = row_inv[...]
    portion = row_in[2, pl.ds(p, 1)] + row_in[2, pl.ds(np_ + p, 1)]
    row_inv[...] = portion[0] * inverse
    logs = [jnp.log(jnp.sum(exp_in[:, c], axis=0)) for c in range(crops)]
    shared = functools.reduce(lambda x, y: x + y, logs[2:])
    lossv = row_inv[pl.ds(core * WIDE, 1)] * (logs[1] + shared)
    lossv = lossv + row_inv[pl.ds(core * WIDE + 1, 1)] * (logs[0] + shared)
    for lane in range(0, WIDTH, 128):
        lossv = lossv - loss_cols[:, lane : lane + 128] * (1.0 / factor)
    loss_out[0] = lossv
    send(plane_peers, loss_out.at[0], loss_plane.at[here], ex_send.at[7], ex_recv.at[7])

    def tail(k, carry):
        serve_all(k)
        return carry

    middle = steps + GROUPS + LAG
    lax.fori_loop(steps + GROUPS, middle, tail, 0)
    await_all(loss_plane, plane, ex_recv.at[7])
    loss_plane[pl.ds(here, 1)] = loss_out[0][None]
    loss_out[1] = jnp.sum(loss_plane[...], axis=0)
    send(z_peers, loss_out.at[1], loss_z.at[z], ex_send.at[8], ex_recv.at[8])
    lax.fori_loop(middle, steps + LAG * hops[0] + 1, tail, 0)

    await_all(loss_z, nz, ex_recv.at[8])
    loss_z[pl.ds(z, 1)] = loss_out[1][None]
    total = jnp.sum(loss_z[...], axis=0)
    loss_ref[...] = jnp.sum(total, axis=1, keepdims=True) * (1.0 / (images_all * PAIRS))

    mine = pl.ds(pl.multiple_of(p * own, own), own)
    for group in range(GROUPS):
        low = group * size
        await_all(cot_in.at[group], np_, cot_recv.at[group])
        cot_in[group, pl.ds(p, 1)] = cot[low : low + size, mine][None]
        total = jnp.sum(cot_in[group], axis=0)
        values = sraw[low : low + size, mine]
        inverse = inverse_norm(jnp.sum(values * values, axis=2, keepdims=True))
        unit = values * inverse
        gf_ref[low : low + size] = inverse * (total - unit * jnp.sum(unit * total, axis=2, keepdims=True))

    for it in range(SK_ITERS):
        await_all(mass_in.at[it], nz, ex_send.at[it])
        await_all(row_in.at[it], plane, ex_send.at[3 + it])
    await_all(exp_in, np_, ex_send.at[6])
    await_all(loss_plane, plane, ex_send.at[7])
    await_all(loss_z, nz, ex_send.at[8])
    teacher_copy.wait_send()
    column_copy.wait_send()
    for group in range(GROUPS):
        await_all(cot_in.at[group], np_, cot_send.at[group])

    def sent(t, carry):
        core_copy(t).wait_send()
        for side in range(2):
            for s in range(hops[side]):
                ring_copy(t, side, s).wait_send()
        return carry

    lax.fori_loop(0, steps, sent, 0)


def on_device(student_features, teacher_features, student_prototypes, teacher_prototypes):
    crops, images, depth = student_features.shape
    columns = student_prototypes.shape[1]
    nb, np_ = lax.axis_size("batch"), lax.axis_size("proto")
    nz = nb // CORES
    rows, trows = crops * images, WIDE * images
    steps, deep, half = columns // WIDTH, depth // nb, columns // CORES
    lanes, own = half // 128, images // np_
    vmem = pltpu.VMEM
    dma = pltpu.SemaphoreType.DMA
    loss, grad_features, grad_prototypes = pl.pallas_call(
        functools.partial(kernel, nb, np_),
        out_shape=(
            jax.ShapeDtypeStruct((1, 1), F32),
            jax.ShapeDtypeStruct((crops, own, depth), F32),
            jax.ShapeDtypeStruct((deep, columns), F32),
        ),
        in_specs=[pl.BlockSpec(memory_space=pl.ANY)] * 4,
        out_specs=[pl.BlockSpec(memory_space=vmem)] * 3,
        scratch_shapes=[
            vmem((rows, depth), BF16),
            vmem((trows, depth), BF16),
            vmem((depth, columns), BF16),
            vmem((depth, columns), BF16),
            vmem((2, trows, depth), BF16),
            vmem((trows, depth), F32),
            vmem((trows, depth), F32),
            vmem((3, trows, half), F32),
            vmem((rows, columns), F32),
            vmem((trows, columns), F32),
            vmem((crops, images, depth), F32),
            vmem((rows, depth), BF16),
            vmem((depth, rows), BF16),
            vmem((2 * trows, depth), BF16),
            vmem((1, columns), F32),
            vmem((rows, 128), F32),
            vmem((rows, 128), F32),
            vmem((rows, columns), BF16),
            vmem((crops, images, depth), F32),
            vmem((GROUPS, np_, crops // GROUPS, own, depth), F32),
            vmem((steps, nz, CORES, deep, WIDTH), F32),
            vmem((steps, nz, deep, WIDTH), F32),
            vmem((steps, 2, nz // 2, deep, WIDTH), F32),
            vmem((2, trows, 128), F32),
            vmem((SK_ITERS, lanes, 128), F32),
            vmem((SK_ITERS, nz, lanes, 128), F32),
            vmem((SK_ITERS, CORES, lanes, 128), F32),
            vmem((SK_ITERS, CORES * WIDE, 128), F32),
            vmem((SK_ITERS, CORES * np_, CORES * WIDE, 128), F32),
            vmem((CORES * WIDE, 128), F32),
            vmem((crops, 1, images), F32),
            vmem((np_, crops, 1, images), F32),
            vmem((1, WIDTH), F32),
            vmem((2, 1, 128), F32),
            vmem((CORES * np_, 1, 128), F32),
            vmem((nz, 1, 128), F32),
            dma((5,)),
            dma((11,)),
            dma((11,)),
            dma((GROUPS,)),
            dma((GROUPS,)),
            dma((steps,)),
            dma((steps,)),
            dma((steps, 2, nz // 2)),
            dma((steps, 2, nz // 2)),
        ],
        compiler_params=pltpu.CompilerParams(
            collective_id=0, has_side_effects=True, vmem_limit_bytes=63 * 1024 * 1024
        ),
    )(
        student_features.reshape(rows, depth),
        teacher_features.reshape(trows, depth),
        student_prototypes,
        teacher_prototypes,
    )
    return loss[0, 0], grad_features, grad_prototypes


def solution(mesh):
    return jax.shard_map(
        on_device,
        mesh=mesh,
        in_specs=(P(None, "batch", None), P(None, "batch", None), P(None, "proto"), P(None, "proto")),
        out_specs=(P(), P(None, ("batch", "proto"), None), P("batch", "proto")),
        check_vma=False,
    )
```

time: 122 us -> 93.5 us (0.77)
  Pallas kernels: 116 us -> 86.7 us
    pallas_call x1, Pallas kernels: 116 us -> 86.7 us  [on_device(): pl.pallas_call(functools.partial(kernel, nb, np_), out_shape=(jax.ShapeDt...]
where the time goes in v2:
time: 93.5 us; the launch traced here: 92.3 us
  Pallas kernels  86.7 us (93%)
  local copies, waits for them, and re-layouts  3.2 us (3%)
  between operations  2.39 us (3%)
    pallas_call x1, Pallas kernels, on_device(): pl.pallas_call(functools.partial(kernel, nb, np_), out_shape=(jax.ShapeDt...  86.7 us
    unnamed x2, local copies, waits for them, and re-layouts  3.2 us

profile of v2, /device:TPU:32, one launch (start us, length us, event | category | flops | bytes accessed | tf_op | source)
XLA Modules:
  0.0 92.3 jit_solution(8124466366660211027)
XLA Ops:
  0.6 86.7 %shard_map.67 = (f32[1,1]{1,0:T(1,128)}, f32[10,8,256]{2,1,0:T(8,128)}, f32[16,4096]{1,0:T(8,128)}) custom-call(bf16[1280,256]{1,0:T(8,128)(2,1)} %bitcast.3, bf16[256,256]{1,0:T(8,128)(2,1)} %bitcast.4, bf16[256,4096]{1,0:T(8,128)(2,1)} %sp_hbm.1, bf16[256,4096]{1,0:T(8,128)(2,1)} %tp_hbm.1), custom_call_target="tpu_custom_call" | custom-call | tf_op jit(solution)/shard_map/pallas_call | solution.py:512
  88.0 1.5 %copy.11 = f32[10,8,256]{2,1,0:T(8,128)} copy(f32[10,8,256]{2,1,0:T(8,128)} %get-tuple-element.13) | data formatting | bytes 163840
  89.5 1.7 %copy.12 = f32[16,4096]{1,0:T(8,128)} copy(f32[16,4096]{1,0:T(8,128)} %get-tuple-element.14) | data formatting | bytes 524288

commit v3 on v2

--- a/solution.py
+++ b/solution.py
@@ -22,6 +22,8 @@
 PART = 256
 LAG = 4
 GROUPS = 2
+BURST = 3
+EACH = 5
 
 
 def inverse_norm(squares):
@@ -104,10 +106,16 @@
     here = core * np_ + p
     hops = (nz // 2, nz - 1 - nz // 2)
 
-    z_peers = [{"batch": lax.rem(z + k, nz) * CORES + core} for k in range(1, nz)]
-    proto_peers = [lax.rem(p + k, np_) for k in range(1, np_)]
-    plane_peers = [{"proto": q} for q in proto_peers]
-    plane_peers += [{"batch": z * CORES + other, "proto": q} for q in proto_peers]
+    far = sorted(range(1, nz), key=lambda k: -min(k, nz - k))
+    z_peers = [{"batch": lax.rem(z + k, nz) * CORES + core} for k in far]
+    side = math.isqrt(np_)
+    y, x = lax.div(p, side), lax.rem(p, side)
+    offsets = [(dy, dx) for dy in range(np_ // side) for dx in range(side)][1:]
+    offsets.sort(key=lambda o: -min(o[0], np_ // side - o[0]) - min(o[1], side - o[1]))
+    proto_peers = [lax.rem(y + dy, np_ // side) * side + lax.rem(x + dx, side) for dy, dx in offsets]
+    plane_peers = []
+    for q in proto_peers:
+        plane_peers += [{"batch": z * CORES + other, "proto": q}, {"proto": q}]
     plane_peers += [{"batch": z * CORES + other}]
 
     def send(peers, source, target, sends, receives):
@@ -284,7 +292,7 @@
     def send_exponentials():
         for c in range(crops):
             exp_out[c] = jnp.sum(racc[c * images : (c + 1) * images, :].T, axis=0, keepdims=True)
-        send(plane_peers[: np_ - 1], exp_out, exp_in.at[p], ex_send.at[6], ex_recv.at[6])
+        send([{"proto": q} for q in proto_peers], exp_out, exp_in.at[p], ex_send.at[6], ex_recv.at[6])
 
     def student_scales():
         await_all(exp_in, np_, ex_recv.at[6])
@@ -295,6 +303,13 @@
             scale[c * images : (c + 1) * images, :] = jnp.broadcast_to(
                 (pairs * factor) / total, (128, images)
             ).T
+
+        def body(j, carry):
+            at = pl.ds(pl.multiple_of(j * 128, 128), 128)
+            expo[:, at] = expo[:, at] * scale[...]
+            return carry
+
+        lax.fori_loop(0, columns // 128, body, 0)
 
     send_mass(0)
     loads[2].wait()
@@ -406,8 +421,7 @@
         for c in range(crops):
             own_rows = slice(c * images, (c + 1) * images)
             target = second if c == 0 else first if c == 1 else both
-            scales = jnp.concatenate([scale[own_rows, :]] * (WIDTH // 128), axis=1)
-            grad[own_rows, at] = (expo[own_rows, at] * scales - target).astype(BF16)
+            grad[own_rows, at] = (expo[own_rows, at] - target).astype(BF16)
         product = jnp.dot(st[...], grad[:, at], preferred_element_type=F32)
         unit = sp_ref[:, at].astype(F32) * pscale[:, at]
         curvature = jnp.sum(pbf[:, at].astype(F32) * product, axis=0, keepdims=True)
@@ -419,6 +433,30 @@
     lax.fori_loop(0, steps, gradient_step, 0)
 
     size = crops // GROUPS
+
+    def send_cot(i):
+        group = lax.div(i, np_ - 1)
+        q = lax.rem(p + 1 + lax.rem(i, np_ - 1), np_)
+        pltpu.make_async_remote_copy(
+            cot.at[
+                pl.ds(group * size, size), pl.ds(pl.multiple_of(q * own, own), own)
+            ],
+            cot_in.at[group, p],
+            cot_send.at[group],
+            cot_recv.at[group],
+            device_id={"proto": q},
+            device_id_type=MESH,
+        ).start()
+
+    def send_more(k):
+        rest = max(np_ - 1 - BURST, 0)
+        for u in range(EACH):
+            n = (k - steps - GROUPS) * EACH + u
+
+            @pl.when(n < GROUPS * rest)
+            def _():
+                send_cot(lax.div(n, rest) * (np_ - 1) + BURST + lax.rem(n, rest))
+
     for group in range(GROUPS):
         low = group * size
         cot[low : low + size] = lax.dot_general(
@@ -427,15 +465,8 @@
             (((1,), (1,)), ((), ())),
             preferred_element_type=F32,
         ).reshape(size, images, depth)
-        for q in proto_peers:
-            pltpu.make_async_remote_copy(
-                cot.at[low : low + size, pl.ds(pl.multiple_of(q * own, own), own)],
-                cot_in.at[group, p],
-                cot_send.at[group],
-                cot_recv.at[group],
-                device_id={"proto": q},
-                device_id_type=MESH,
-            ).start()
+        for k in range(min(BURST, np_ - 1)):
+            send_cot(group * (np_ - 1) + k)
         serve_all(steps + group)
 
     inverse = row_inv[...]
@@ -452,6 +483,8 @@
 
     def tail(k, carry):
         serve_all(k)
+        if np_ - 1 > BURST:
+            send_more(k)
         return carry
 
     middle = steps + GROUPS + LAG
@@ -497,6 +530,11 @@
         return carry
 
     lax.fori_loop(0, steps, sent, 0)
+
+
+def hand_on(*refs):
+    for source, target in zip(refs[:3], refs[3:]):
+        target[...] = source[...]
 
 
 def on_device(student_features, teacher_features, student_prototypes, teacher_prototypes):
@@ -574,6 +612,12 @@
         student_prototypes,
         teacher_prototypes,
     )
+    loss, grad_features, grad_prototypes = pl.pallas_call(
+        hand_on,
+        out_shape=[jax.ShapeDtypeStruct(r.shape, r.dtype) for r in (loss, grad_features, grad_prototypes)],
+        in_specs=[pl.BlockSpec(memory_space=vmem)] * 3,
+        out_specs=[pl.BlockSpec(memory_space=vmem)] * 3,
+    )(loss, grad_features, grad_prototypes)
     return loss[0, 0], grad_features, grad_prototypes
 
 

time: 93.5 us -> 85.3 us (0.912); the launches traced: 92.3 us -> 85.2 us
  local copies, waits for them, and re-layouts: 3.2 us -> 0 us
  Pallas kernels: 86.7 us -> 84.6 us
  between operations: 2.39 us -> 0.64 us
    pallas_call x1, Pallas kernels: 86.7 us -> 82.2 us  [on_device(): pl.pallas_call(functools.partial(kernel, nb, np_), out_shape=(jax.ShapeDt...]
    unnamed x2 -> x0, local copies, waits for them, and re-layouts: 3.2 us -> none
    pallas_call x0 -> x1, Pallas kernels: none -> 2.37 us  [on_device(): pl.pallas_call(hand_on, out_shape=[jax.ShapeDtypeStruct(r.shape, r.dtype)...]
where the time goes in v3:
time: 85.3 us; the launch traced here: 85.2 us
  Pallas kernels  84.6 us (99%)
    pallas_call x1, Pallas kernels, on_device(): pl.pallas_call(functools.partial(kernel, nb, np_), out_shape=(jax.ShapeDt...  82.2 us
    pallas_call x1, Pallas kernels, on_device(): pl.pallas_call(hand_on, out_shape=[jax.ShapeDtypeStruct(r.shape, r.dtype)...  2.37 us

profile of v3, /device:TPU:32, one launch (start us, length us, event | category | flops | bytes accessed | tf_op | source)
XLA Modules:
  0.0 85.2 jit_solution(12302816008517995027)
XLA Ops:
  0.6 82.2 %shard_map.67 = (f32[1,1]{1,0:T(1,128)}, f32[10,8,256]{2,1,0:T(8,128)}, f32[16,4096]{1,0:T(8,128)}) custom-call(bf16[1280,256]{1,0:T(8,128)(2,1)} %bitcast.3, bf16[256,256]{1,0:T(8,128)(2,1)} %bitcast.4, bf16[256,4096]{1,0:T(8,128)(2,1)} %sp_hbm.1, bf16[256,4096]{1,0:T(8,128)(2,1)} %tp_hbm.1), custom_call_target="tpu_custom_call" | custom-call | tf_op jit(solution)/shard_map/pallas_call | solution.py:550
  82.9 2.4 %shard_map.68 = (f32[1,1]{1,0:T(1,128)}, f32[10,8,256]{2,1,0:T(8,128)}, f32[16,4096]{1,0:T(8,128)}) custom-call(f32[1,1]{1,0:T(1,128)} %get-tuple-element.9.refs_0_, f32[10,8,256]{2,1,0:T(8,128)} %get-tuple-element.10.refs_1_, f32[16,4096]{1,0:T(8,128)} %get-tuple-element.11.refs_2_), custom_call_target="tpu_custom_call" | custom-call | tf_op jit(solution)/shard_map/pallas_call | solution.py:615

commit v4 on v3

--- a/solution.py
+++ b/solution.py
@@ -20,7 +20,8 @@
 BF16 = jnp.bfloat16
 WIDTH = 512
 PART = 256
-LAG = 4
+FIRST = 2
+LAG = 3
 GROUPS = 2
 BURST = 3
 EACH = 5
@@ -139,10 +140,10 @@
         pltpu.make_async_copy(sp_hbm, sp_ref, load_sem.at[4]),
     ]
     barrier = pltpu.get_barrier_semaphore()
+    for load in loads:
+        load.start()
     for peer in z_peers + plane_peers:
         pl.semaphore_signal(barrier, inc=1, device_id=peer, device_id_type=MESH)
-    for load in loads:
-        load.start()
 
     loads[0].wait()
     values = tf_ref[...].astype(F32)
@@ -179,8 +180,6 @@
             mass_out[0, pl.ds(j * (PART // 128) + lane, 1)] = mass[:, lane * 128 : (lane + 1) * 128]
         return carry
 
-    loads[1].wait()
-    lax.fori_loop(0, half // PART // 2, own_half, 0)
     pl.semaphore_wait(barrier, nz - 1 + plane - 1)
     teacher_copy = pltpu.make_async_remote_copy(
         tsend,
@@ -191,7 +190,8 @@
         device_id_type=MESH,
     )
     teacher_copy.start()
-    lax.fori_loop(half // PART // 2, half // PART, own_half, 0)
+    loads[1].wait()
+    lax.fori_loop(0, half // PART, own_half, 0)
     teacher_copy.wait_recv()
     tbf[1] = trecv[...].astype(BF16)
     lax.fori_loop(0, half // PART, other_rows, 0)
@@ -400,7 +400,7 @@
 
     def serve_all(k):
         for phase in range(hops[0], -1, -1):
-            t = k - 1 - LAG * phase
+            t = k - FIRST - LAG * phase
 
             @pl.when(jnp.logical_and(t >= 0, t < steps))
             def _():
@@ -493,7 +493,7 @@
     loss_plane[pl.ds(here, 1)] = loss_out[0][None]
     loss_out[1] = jnp.sum(loss_plane[...], axis=0)
     send(z_peers, loss_out.at[1], loss_z.at[z], ex_send.at[8], ex_recv.at[8])
-    lax.fori_loop(middle, steps + LAG * hops[0] + 1, tail, 0)
+    lax.fori_loop(middle, steps + LAG * hops[0] + FIRST, tail, 0)
 
     await_all(loss_z, nz, ex_recv.at[8])
     loss_z[pl.ds(z, 1)] = loss_out[1][None]

time: 85.3 us -> 84.5 us (level)
  Pallas kernels: 84.6 us -> 83.1 us
    pallas_call x1, Pallas kernels: 82.2 us -> 80.7 us  [on_device(): pl.pallas_call(functools.partial(kernel, nb, np_), out_shape=(jax.ShapeDt...]
where the time goes in v4:
time: 84.5 us; the launch traced here: 83.7 us
  Pallas kernels  83.1 us (98%)
    pallas_call x1, Pallas kernels, on_device(): pl.pallas_call(functools.partial(kernel, nb, np_), out_shape=(jax.ShapeDt...  80.7 us
    pallas_call x1, Pallas kernels, on_device(): pl.pallas_call(hand_on, out_shape=[jax.ShapeDtypeStruct(r.shape, r.dtype)...  2.37 us

profile of v4, /device:TPU:32, one launch (start us, length us, event | category | flops | bytes accessed | tf_op | source)
XLA Modules:
  0.0 83.7 jit_solution(6598929825030454306)
XLA Ops:
  0.6 80.7 %shard_map.67 = (f32[1,1]{1,0:T(1,128)}, f32[10,8,256]{2,1,0:T(8,128)}, f32[16,4096]{1,0:T(8,128)}) custom-call(bf16[1280,256]{1,0:T(8,128)(2,1)} %bitcast.3, bf16[256,256]{1,0:T(8,128)(2,1)} %bitcast.4, bf16[256,4096]{1,0:T(8,128)(2,1)} %sp_hbm.1, bf16[256,4096]{1,0:T(8,128)(2,1)} %tp_hbm.1), custom_call_target="tpu_custom_call" | custom-call | tf_op jit(solution)/shard_map/pallas_call | solution.py:550
  81.3 2.4 %shard_map.68 = (f32[1,1]{1,0:T(1,128)}, f32[10,8,256]{2,1,0:T(8,128)}, f32[16,4096]{1,0:T(8,128)}) custom-call(f32[1,1]{1,0:T(1,128)} %get-tuple-element.9.refs_0_, f32[10,8,256]{2,1,0:T(8,128)} %get-tuple-element.10.refs_1_, f32[16,4096]{1,0:T(8,128)} %get-tuple-element.11.refs_2_), custom_call_target="tpu_custom_call" | custom-call | tf_op jit(solution)/shard_map/pallas_call | solution.py:615

commit v5 on v4

--- a/solution.py
+++ b/solution.py
@@ -385,6 +385,7 @@
             for side in range(2):
                 if hops[side]:
                     ring_copy(t, side, 0).start()
+            core_copy(t).wait_send()
             return
         s = phase - 1
         for side in range(2):
@@ -394,6 +395,7 @@
                 wt[t, segment, core] += wt_ring[t, side, s]
                 if s + 1 < hops[side]:
                     ring_copy(t, side, s + 1).start()
+                ring_copy(t, side, s).wait_send()
         if s + 1 == hops[0]:
             at = pl.ds(pl.multiple_of(t * WIDTH, WIDTH), WIDTH)
             gp_ref[:, at] = pscale[:, at] * wt[t, z, core]
@@ -469,6 +471,13 @@
             send_cot(group * (np_ - 1) + k)
         serve_all(steps + group)
 
+    for it in range(SK_ITERS):
+        await_all(mass_in.at[it], nz, ex_send.at[it])
+        await_all(row_in.at[it], plane, ex_send.at[3 + it])
+    await_all(exp_in, np_, ex_send.at[6])
+    teacher_copy.wait_send()
+    column_copy.wait_send()
+
     inverse = row_inv[...]
     portion = row_in[2, pl.ds(p, 1)] + row_in[2, pl.ds(np_ + p, 1)]
     row_inv[...] = portion[0] * inverse
@@ -511,25 +520,10 @@
         unit = values * inverse
         gf_ref[low : low + size] = inverse * (total - unit * jnp.sum(unit * total, axis=2, keepdims=True))
 
-    for it in range(SK_ITERS):
-        await_all(mass_in.at[it], nz, ex_send.at[it])
-        await_all(row_in.at[it], plane, ex_send.at[3 + it])
-    await_all(exp_in, np_, ex_send.at[6])
     await_all(loss_plane, plane, ex_send.at[7])
     await_all(loss_z, nz, ex_send.at[8])
-    teacher_copy.wait_send()
-    column_copy.wait_send()
     for group in range(GROUPS):
         await_all(cot_in.at[group], np_, cot_send.at[group])
-
-    def sent(t, carry):
-        core_copy(t).wait_send()
-        for side in range(2):
-            for s in range(hops[side]):
-                ring_copy(t, side, s).wait_send()
-        return carry
-
-    lax.fori_loop(0, steps, sent, 0)
 
 
 def hand_on(*refs):

time: 84.5 us -> 84.4 us (level)
  no operation moved by 1% of the time
where the time goes in v5:
time: 84.4 us; the launch traced here: 83.6 us
  Pallas kernels  83 us (98%)
    pallas_call x1, Pallas kernels, on_device(): pl.pallas_call(functools.partial(kernel, nb, np_), out_shape=(jax.ShapeDt...  80.6 us
    pallas_call x1, Pallas kernels, on_device(): pl.pallas_call(hand_on, out_shape=[jax.ShapeDtypeStruct(r.shape, r.dtype)...  2.37 us

profile of v5, /device:TPU:32, one launch (start us, length us, event | category | flops | bytes accessed | tf_op | source)
XLA Modules:
  0.0 83.6 jit_solution(8791825022084958407)
XLA Ops:
  0.6 80.6 %shard_map.67 = (f32[1,1]{1,0:T(1,128)}, f32[10,8,256]{2,1,0:T(8,128)}, f32[16,4096]{1,0:T(8,128)}) custom-call(bf16[1280,256]{1,0:T(8,128)(2,1)} %bitcast.3, bf16[256,256]{1,0:T(8,128)(2,1)} %bitcast.4, bf16[256,4096]{1,0:T(8,128)(2,1)} %sp_hbm.1, bf16[256,4096]{1,0:T(8,128)(2,1)} %tp_hbm.1), custom_call_target="tpu_custom_call" | custom-call | tf_op jit(solution)/shard_map/pallas_call | solution.py:544
  81.2 2.4 %shard_map.68 = (f32[1,1]{1,0:T(1,128)}, f32[10,8,256]{2,1,0:T(8,128)}, f32[16,4096]{1,0:T(8,128)}) custom-call(f32[1,1]{1,0:T(1,128)} %get-tuple-element.9.refs_0_, f32[10,8,256]{2,1,0:T(8,128)} %get-tuple-element.10.refs_1_, f32[16,4096]{1,0:T(8,128)} %get-tuple-element.11.refs_2_), custom_call_target="tpu_custom_call" | custom-call | tf_op jit(solution)/shard_map/pallas_call | solution.py:609
